TPU v7x, 32 devices: a whole 2x2x4 slice. The times are simulated.
32 devices in a mesh: dp: 4 (over y, core), seq: 8 (over z, x).
Axes of the slice: x: 2, y: 2, z: 4, core: 2. Of those that a mesh axis runs over, the one named last changes fastest.
Arguments:
- glu_out: bfloat16 [4, 1024, 1536], P('dp', 'seq'), may hold values from -8 to 8
- conv_weight: float32 [32, 1536], replicated, may hold values from -1 to 1
- bn_gain: float32 [16, 1536], replicated, may hold values from 0.25 to 1.75
- bn_bias: float32 [16, 1536], replicated, may hold values from -3 to 3
- w_out: bfloat16 [1536, 1536], P(('dp', 'seq')), may hold values from -0.15625 to 0.15625
- cotangent: bfloat16 [4, 1024, 1536], P('dp', 'seq'), may hold values from -8 to 8
- language: int32 [4], P('dp'), may hold values from 0 to 15
- length: int32 [4], P('dp'), may hold values from 256 to 1024, as said below
Outputs:
- block_out: bfloat16 [4, 1024, 1536], P('dp', 'seq')
- weight_grad: float32 [1536, 1536], P(('dp', 'seq'))
- input_grad: bfloat16 [4, 1024, 1536], P('dp', 'seq')
Inputs may be any that keep to these rules, and one draw needn't show every extreme that they name: Each length is a multiple of 256; at least one utterance is valid over all 1024 frames.
All inputs are finite; a program needn't handle non-finite values.
Results may differ from a plain program's by a relative error of at most 0.0095.
Values may be sent and summed in bfloat16 or wider, within the bound.
A program may use at most 64 MiB of HBM per device.

v0:
```python
import jax
import jax.numpy as jnp
from jax import lax
from jax.sharding import PartitionSpec as P

LANGS = 16


epsilon = 1e-05


def with_halo(array, sides, width):
    for axis, dim in sides:
        size, length = (lax.axis_size(axis), array.shape[dim])
        up = [(i, (i + 1) % size) for i in range(size - 1)]
        down = [(j, i) for i, j in up]
        last = lax.slice_in_dim(array, length - width, length, axis=dim)
        first = lax.slice_in_dim(array, 0, width, axis=dim)
        before = lax.ppermute(last, axis, up)
        after = lax.ppermute(first, axis, down)
        array = jnp.concatenate([before, array, after], axis=dim)
    return array


def depthwise(padded, taps, frames):
    running = jnp.zeros((padded.shape[0], frames, padded.shape[2]), jnp.float32)
    for offset in range(taps.shape[0]):
        running = running + padded[:, offset : offset + frames].astype(jnp.float32) * taps[offset]
    return running


def with_rim(values, half_width):
    return with_halo(values, (("seq", 1),), half_width)


def per_language(one_hot, values_table):
    return jnp.dot(one_hot.T, values_table, precision=lax.Precision.HIGHEST)


def per_utterance(one_hot, values_table):
    return jnp.dot(one_hot, values_table, precision=lax.Precision.HIGHEST)[:, None, :]


def on_device(glu_out, conv_weight, bn_gain, bn_bias, w_out, cotangent, language, length):
    utterances, frames, channels = glu_out.shape
    kernel = conv_weight.shape[0]
    half_width = kernel // 2
    position = lax.axis_index("seq") * frames + lax.iota(jnp.int32, frames)
    valid = (position[None, :] < length[:, None]).astype(jnp.float32)[:, :, None]
    one_hot = (language[:, None] == lax.iota(jnp.int32, LANGS)[None, :]).astype(jnp.float32)
    masked = glu_out * valid.astype(jnp.bfloat16)
    extended = with_rim(masked, half_width)
    convolved = depthwise(extended[:, : frames + kernel - 1], conv_weight, frames)
    counts = per_language(one_hot, jnp.sum(valid, axis=(1, 2)))
    local_sum = per_language(one_hot, jnp.sum(convolved * valid, axis=1))
    local_square = per_language(one_hot, jnp.sum(convolved * convolved * valid, axis=1))
    total_sum, total_square, total_count = lax.psum(
        (local_sum, local_square, counts), ("dp", "seq")
    )
    denominator = jnp.maximum(total_count, 1.0)[:, None]
    average = total_sum / denominator
    variance = total_square / denominator - average * average
    average_utt = per_utterance(one_hot, average)
    inverse_utt = per_utterance(one_hot, lax.rsqrt(variance + epsilon))
    gain_utt = per_utterance(one_hot, bn_gain)
    bias_utt = per_utterance(one_hot, bn_bias)
    normed = (convolved - average_utt) * inverse_utt
    pre_act = normed * gain_utt + bias_utt
    sigmoid_act = jax.nn.sigmoid(pre_act)
    active = (pre_act * sigmoid_act * valid).astype(jnp.bfloat16)
    full_weight = lax.all_gather(w_out, ("dp", "seq"), axis=0, tiled=True)
    flat_active = active.reshape(utterances * frames, channels)
    flat_grad = cotangent.reshape(utterances * frames, channels)
    output = jnp.dot(flat_active, full_weight, preferred_element_type=jnp.float32)
    output = output.astype(jnp.bfloat16).reshape(utterances, frames, channels)
    back_proj = lax.dot_general(
        flat_grad, full_weight, (((1,), (1,)), ((), ())), preferred_element_type=jnp.float32
    )
    back_proj = back_proj.reshape(utterances, frames, channels)
    grad_pre = back_proj * valid * sigmoid_act * (1.0 + pre_act * (1.0 - sigmoid_act))
    grad_normed = grad_pre * gain_utt
    first_sum, second_sum = lax.psum(
        (
            per_language(one_hot, jnp.sum(grad_normed, axis=1)),
            per_language(one_hot, jnp.sum(grad_normed * normed, axis=1)),
        ),
        ("dp", "seq"),
    )
    shift_term = per_utterance(one_hot, first_sum / denominator)
    scale_term = per_utterance(one_hot, second_sum / denominator)
    grad_conv = (valid * inverse_utt * (grad_normed - shift_term - normed * scale_term)).astype(
        jnp.bfloat16
    )
    rim_grad = with_rim(grad_conv, half_width)
    input_grad = (depthwise(rim_grad[:, 1:], conv_weight[::-1], frames) * valid).astype(
        jnp.bfloat16
    )
    weight_grad = lax.psum_scatter(
        lax.dot_general(
            flat_active, flat_grad, (((0,), (0,)), ((), ())), preferred_element_type=jnp.float32
        ),
        ("dp", "seq"),
        scatter_dimension=0,
        tiled=True,
    )
    return (output, weight_grad, input_grad)


def solution(mesh):
    placed = (
        P("dp", "seq", None),
        P(),
        P(),
        P(),
        P(("dp", "seq"), None),
        P("dp", "seq", None),
        P("dp"),
        P("dp"),
    )
    return jax.shard_map(
        on_device,
        mesh=mesh,
        in_specs=placed,
        out_specs=(P("dp", "seq", None), P(("dp", "seq"), None), P("dp", "seq", None)),
        check_vma=False,
    )
```

profile of v0, /device:TPU:0, one launch (start us, length us, event | category | flops | bytes accessed | tf_op | source)
XLA Modules:
  0.0 496.2 jit_solution(14863246846931838560)
XLA Ops:
  7.2 0.0 copy-start
  7.2 0.0 all-reduce.7.cloned.1.call-start
  7.9 0.6 fusion.95
  8.5 1.1 broadcast_multiply_fusion
  9.6 4.8 collective-permute-start
  14.5 1.3 collective-permute-start.1
  15.8 1.5 slice_reduce_fusion.30
  17.3 1.8 slice_reduce_fusion.31
  19.8 0.0 collective-permute-done
  19.8 0.6 collective-permute-done.1
  20.5 3.9 multiply_reduce_fusion.2
  24.4 0.8 broadcast_multiply_fusion.4
  25.1 0.0 all-reduce.7.cloned.1.call-update
  25.1 0.0 all-gather.2.cloned.1.call-start
  25.2 0.7 all-gather.2.cloned.1.call-update
  25.9 0.0 all-reduce.5.cloned.1.call-start
  25.9 0.7 fusion.85
  26.6 41.5 %psum.36 = f32[16]{0:T(128)S(1)} all-reduce(f32[16]{0:T(128)S(1)} %fusion.85), channel_id=1, replica_groups=mesh['dp'=4,'seq'=8] {'dp','seq'}, use_global_device_ids=true, to_apply=%region_3.0 | all-reduce | flops 16 | bytes 128 | tf_op jit(solution)/shard_map/psum | solution.py:57
  68.1 1.1 convolution_reduce_fusion.3
  69.1 1.1 convolution_reduce_fusion.2
  70.2 80.4 %all-reduce.7.cloned.1.call-done = (f32[16,1536]{1,0:T(8,128)}, f32[16,1536]{1,0:T(8,128)}) async-done(((f32[16,1536]{1,0:T(8,128)}, f32[16,1536]{1,0:T(8,128)}), (f32[16,1536]{1,0:T(8,128)}, f32[16,1536]{1,0:T(8,128)})) %all-reduce.7.cloned.1.call-update) | async-done | bytes 196624 | tf_op jit(solution)/shard_map/psum | solution.py:57
  150.6 1.1 convolution_reduce_fusion.5
  151.8 1.2 convolution_reduce_fusion.4
  153.0 65.3 %all-gather.2.cloned.1.call-done = bf16[1536,1536]{1,0:T(8,128)(2,1)} async-done(((bf16[48,1536]{1,0:T(8,128)(2,1)}), bf16[1536,1536]{1,0:T(8,128)(2,1)}) %all-gather.2.cloned.1.call-update) | async-done | bytes 4718608 | tf_op jit(solution)/shard_map/all_gather | solution.py:71
  218.3 0.0 copy-done
  218.3 4.1 fusion.94
  222.4 0.8 broadcast_multiply_fusion.2
  223.2 0.0 all-reduce.5.cloned.1.call-update
  223.2 0.0 reduce-scatter.2.cloned.1.call-start
  223.2 5.2 %fusion.64 = f32[1536,1536]{1,0:T(8,128)} fusion(bf16[1,128,1536]{2,1,0:T(8,128)(2,1)S(1)} %copy-done, f32[1,128,1536]{2,1,0:T(8,128)S(1)} %get-tuple-element.45, f32[1536]{0:T(1024)S(1)} %convolution_reduce_fusion.2, f32[1536]{0:T(1024)S(1)} %convolution_reduce_fusion.3, f32[1536]{0:T(1024)S(1)} %convolution_reduce_fusion.4, ...), kind=kOutput, calls=%fused_computation.185 | convolution fusion | flops 605945856 | bytes 10641920 | tf_op jit(solution)/shard_map/dot_general | solution.py:99
  228.4 0.0 reduce-scatter.2.cloned.1.call-update
  228.4 118.3 %all-reduce.5.cloned.1.call-done = (f32[16,1536]{1,0:T(8,128)}, f32[16,1536]{1,0:T(8,128)}) async-done(((f32[16,1536]{1,0:T(8,128)}, f32[16,1536]{1,0:T(8,128)}), (f32[16,1536]{1,0:T(8,128)}, f32[16,1536]{1,0:T(8,128)})) %all-reduce.5.cloned.1.call-update) | async-done | bytes 196624 | tf_op jit(solution)/shard_map/psum | solution.py:82
  346.7 1.1 convolution_reduce_fusion
  347.9 1.1 convolution_reduce_fusion.1
  349.0 0.3 multiply_convert_fusion.1
  349.3 1.3 collective-permute-start.3
  350.6 4.5 collective-permute-start.2
  355.2 4.0 fusion.4
  359.1 0.0 collective-permute-done.3
  359.2 0.0 collective-permute-done.2
  359.2 4.5 multiply_convert_fusion
  363.6 126.0 %reduce-scatter.2.cloned.1.call-done = f32[48,1536]{1,0:T(8,128)} async-done(((f32[1536,1536]{1,0:T(8,128)}), f32[48,1536]{1,0:T(8,128)}) %reduce-scatter.2.cloned.1.call-update) | async-done | bytes 294928 | tf_op jit(solution)/shard_map/reduce_scatter | solution.py:98
  (5 shorter events, 0.0 us)
Async XLA Ops:
  7.2 211.1 %copy-start = (bf16[1,128,1536]{2,1,0:T(8,128)(2,1)S(1)}, bf16[1,128,1536]{2,1,0:T(8,128)(2,1)}, u32[]{:S(2)}) copy-start(bf16[1,128,1536]{2,1,0:T(8,128)(2,1)} %param.13) | copy-start | bytes 1179652
  7.2 143.5 %all-reduce.7.cloned.1.call-start = ((), (), s32[]{:S(2)}) async-start(), calls=%async_computation.4 | async-start | bytes 393216 | tf_op jit(solution)/shard_map/psum | solution.py:57
  9.6 10.2 %collective-permute-start = (bf16[1,16,1536]{2,1,0:T(8,128)(2,1)S(1)}, bf16[1,16,1536]{2,1,0:T(8,128)(2,1)S(1)}, u32[]{:S(2)}, u32[]{:S(2)}) collective-permute-start(bf16[1,16,1536]{2,1,0:T(8,128)(2,1)S(1)} %get-tuple-element.48), channel_id=1, source_target_pairs={{0,1},{1,2},{2,3},{3,4},{4,5},{5,6},{6,7},{8,9},{9,10},{10,11},{11... | collective-permute-start | bytes 147464 | tf_op jit(solution)/shard_map/ppermute | solution.py:19
  14.5 6.0 %collective-permute-start.1 = (bf16[1,16,1536]{2,1,0:T(8,128)(2,1)S(1)}, bf16[1,16,1536]{2,1,0:T(8,128)(2,1)S(1)}, u32[]{:S(2)}, u32[]{:S(2)}) collective-permute-start(bf16[1,16,1536]{2,1,0:T(8,128)(2,1)S(1)} %get-tuple-element.49), channel_id=1, source_target_pairs={{1,0},{2,1},{3,2},{4,3},{5,4},{6,5},{7,6},{9,8},{10,9},{11,10},{12... | collective-permute-start | bytes 147464 | tf_op jit(solution)/shard_map/ppermute | solution.py:20
  25.1 193.1 %all-gather.2.cloned.1.call-start = ((), (), s32[]{:S(2)}) async-start(), calls=%async_computation.1 | async-start | bytes 4866048 | tf_op jit(solution)/shard_map/all_gather | solution.py:71
  25.9 320.8 %all-reduce.5.cloned.1.call-start = ((), (), s32[]{:S(2)}) async-start(), calls=%async_computation.3 | async-start | bytes 393216 | tf_op jit(solution)/shard_map/psum | solution.py:82
  223.2 266.4 %reduce-scatter.2.cloned.1.call-start = ((), (), s32[]{:S(2)}) async-start(), calls=%async_computation.2 | async-start | bytes 9732096 | tf_op jit(solution)/shard_map/reduce_scatter | solution.py:98
  349.3 9.9 %collective-permute-start.3 = (bf16[1,16,1536]{2,1,0:T(8,128)(2,1)S(1)}, bf16[1,16,1536]{2,1,0:T(8,128)(2,1)S(1)}, u32[]{:S(2)}, u32[]{:S(2)}) collective-permute-start(bf16[1,16,1536]{2,1,0:T(8,128)(2,1)S(1)} %get-tuple-element.46), channel_id=1, source_target_pairs={{1,0},{2,1},{3,2},{4,3},{5,4},{6,5},{7,6},{9,8},{10,9},{11,10},{12... | collective-permute-start | bytes 147464 | tf_op jit(solution)/shard_map/ppermute | solution.py:20
  350.6 8.6 %collective-permute-start.2 = (bf16[1,16,1536]{2,1,0:T(8,128)(2,1)S(1)}, bf16[1,16,1536]{2,1,0:T(8,128)(2,1)S(1)}, u32[]{:S(2)}, u32[]{:S(2)}) collective-permute-start(bf16[1,16,1536]{2,1,0:T(8,128)(2,1)S(1)} %get-tuple-element.47), channel_id=1, source_target_pairs={{0,1},{1,2},{2,3},{3,4},{4,5},{5,6},{6,7},{8,9},{9,10},{10,11},{11... | collective-permute-start | bytes 147464 | tf_op jit(solution)/shard_map/ppermute | solution.py:19
Sparse Core Ops, SparseCore 0:
  25.3 125.3 all-reduce.6
  153.6 64.5 all-gather.1
  224.5 122.2 all-reduce.4
  353.1 136.5 reduce-scatter.1
where the time goes:
time: 497 us; the launch traced here: 496 us
  waiting for transfers between devices  391 us (79%)
  blocking collectives  41.5 us (8%)
  matrix products  20 us (4%)
  between operations  15.3 us (3%)
  other arithmetic  12.5 us (3%)
  starting transfers between devices  12.1 us (2%)
    reduce_scatter x1, waiting for transfers between devices, on_device(): lax.psum_scatter(lax.dot_general(flat_active, flat_grad, (((0,), (0,)), (...  126 us
    psum x1, waiting for transfers between devices, on_device(): lax.psum((per_language(one_hot, jnp.sum(grad_normed, axis=1)), per_langua...  118 us
    psum x1, waiting for transfers between devices, on_device(): lax.psum((local_sum, local_square, counts), ('dp', 'seq'))  80.4 us
    all_gather x1, waiting for transfers between devices, on_device(): full_weight = lax.all_gather(w_out, ('dp', 'seq'), axis=0, tiled=True)  65.3 us
    psum x1, blocking collectives, on_device(): lax.psum((local_sum, local_square, counts), ('dp', 'seq'))  41.5 us
  transfers between devices with their start and end apart: 8, of which 5 were waited for; matrix products, arithmetic and copies ran while one was open for 5% of the time, Pallas kernels for 0%

commit v1 on v0

--- a/solution.py
+++ b/solution.py
@@ -1,6 +1,8 @@
 import jax
 import jax.numpy as jnp
 from jax import lax
+from jax.experimental import pallas as pl
+from jax.experimental.pallas import tpu as pltpu
 from jax.sharding import PartitionSpec as P
 
 LANGS = 16
@@ -106,6 +108,329 @@
     return (output, weight_grad, input_grad)
 
 
+MESH = pl.DeviceIdType.MESH
+LANE = 128
+
+
+def tile(c):
+    return pl.ds(pl.multiple_of(c * LANE, LANE), LANE)
+
+
+def fused(
+    lang_ref, len_ref, x_ref, tap_ref, gain_ref, bias_ref, w_ref, cot_ref,
+    out_ref, wg_ref, ig_ref,
+    wfull, cotg, act, act_t, ag, part, ysum, yin, zin,
+    ext, xf, normed, slope, gext,
+    info, info_in, stat, stat_in, stat_mid, stat_dp, stat_res,
+    send, recv,
+):
+    frames, channels = x_ref.shape
+    taps = tap_ref.shape[0]
+    half = taps // 2
+    chunks = channels // LANE
+    dp, seq = lax.axis_index("dp"), lax.axis_index("seq")
+    y, c, z, x = dp // 2, dp % 2, seq // 2, seq % 2
+    seq_x, dp_c, dp_y = seq + 1 - 2 * x, dp + 1 - 2 * c, dp + 2 - 4 * y
+    to_x, to_c, to_y, to_cx = (dp, seq_x), (dp_c, seq), (dp_y, seq), (dp_c, seq_x)
+    xn, cn, yn = 1 - x, 1 - c, 1 - y
+    seq_peers = [(dp, (seq + d) % 8) for d in range(1, 8)]
+    dp_peers = [((dp + d) % 4, seq) for d in range(1, 4)]
+    z_peers = [(z + d) % 4 for d in range(1, 4)]
+    lang, length = lang_ref[0], len_ref[0]
+
+    barrier = pltpu.get_barrier_semaphore()
+    greet = seq_peers + dp_peers + [to_cx]
+    for peer in greet:
+        pl.semaphore_signal(barrier, inc=1, device_id=peer, device_id_type=MESH)
+
+    info[0:8, :] = jnp.full((8, LANE), lang, jnp.int32)
+    info[8:16, :] = jnp.full((8, LANE), length, jnp.int32)
+    wfull[dp, z, x] = w_ref[...]
+    cotg[0] = cot_ref[...]
+    pl.semaphore_wait(barrier, len(greet))
+
+    pending = []
+    count = [0]
+
+    def push(src, dst, peer):
+        i = count[0]
+        count[0] += 1
+        copy = pltpu.make_async_remote_copy(
+            src_ref=src, dst_ref=dst, send_sem=send.at[i], recv_sem=recv.at[i],
+            device_id=peer, device_id_type=MESH,
+        )
+        copy.start()
+        pending.append(copy)
+        return copy
+
+    seq_up, seq_down = (dp, (seq + 1) % 8), (dp, (seq + 7) % 8)
+    halo = [
+        push(x_ref.at[frames - half : frames], ext.at[0:half], seq_up),
+        push(x_ref.at[0:half], ext.at[half + frames : frames + 2 * half], seq_down),
+    ]
+    w_z = [push(w_ref, wfull.at[dp, z, x], (dp, zp * 2 + x)) for zp in z_peers]
+    cot_x = push(cot_ref, cotg.at[1], to_x)
+    cot_c = push(cot_ref, cotg.at[2], to_c)
+    told = [push(info, info_in.at[d], peer) for d, peer in enumerate(dp_peers)]
+
+    row = lax.broadcasted_iota(jnp.int32, (frames + 2 * half, LANE), 0) + (seq * frames - half)
+    inside = (row >= 0) & (row < length)
+    valid = inside[half : half + frames].astype(jnp.float32)
+
+    ext[half : half + frames, :] = x_ref[...]
+    for copy in halo:
+        copy.wait_recv()
+
+    def conv_step(i, carry):
+        t = tile(i)
+        xf[:, t] = jnp.where(inside, ext[:, t].astype(jnp.float32), 0.0)
+        weights = tap_ref[:, t]
+        total = jnp.zeros((frames, LANE), jnp.float32)
+        for k in range(taps):
+            total = total + xf[k : k + frames, t] * weights[k : k + 1]
+        normed[:, t] = total
+        kept = total * valid
+        stat[0, pl.ds(i, 1), :] = jnp.sum(kept, axis=0, keepdims=True)
+        stat[0, pl.ds(chunks + i, 1), :] = jnp.sum(kept * total, axis=0, keepdims=True)
+        return carry
+
+    lax.fori_loop(0, chunks, conv_step, 0)
+
+    def sum_seq(n):
+        return [push(stat.at[n], stat_in.at[n, d], peer) for d, peer in enumerate(seq_peers)]
+
+    def sum_dp(n, copies):
+        for copy in copies:
+            copy.wait_recv()
+        total = stat[n]
+        for d in range(7):
+            total = total + stat_in[n, d]
+        stat_mid[n] = total
+        return [push(stat_mid.at[n], stat_dp.at[n, d], peer) for d, peer in enumerate(dp_peers)]
+
+    def finish(n, copies):
+        for copy in copies:
+            copy.wait_recv()
+        total = stat_mid[n]
+        frames_of = jnp.full((1, LANE), length, jnp.int32).astype(jnp.float32)
+        for d in range(3):
+            same = (info_in[d, 0:1, :] == lang).astype(jnp.float32)
+            total = total + stat_dp[n, d] * same
+            frames_of = frames_of + info_in[d, 8:9, :].astype(jnp.float32) * same
+        return total / jnp.maximum(frames_of, 1.0)
+
+    first = sum_seq(0)
+
+    for copy in w_z:
+        copy.wait_recv()
+    w_x = push(wfull.at[dp, :, x], wfull.at[dp, :, x], to_x)
+    w_y = push(wfull.at[dp, :, x], wfull.at[dp, :, x], to_y)
+    w_core = [push(wfull.at[dp, :, x], wfull.at[dp, :, x], to_c)]
+
+    first = sum_dp(0, first)
+    cot_x.wait_recv()
+    cot_cx = push(cotg.at[1], cotg.at[3], to_c)
+    for copy in told:
+        copy.wait_recv()
+    mean = finish(0, first)
+    average = mean[0:chunks]
+    variance = mean[chunks : 2 * chunks] - average * average
+    stat_res[0, 0:chunks, :] = average
+    stat_res[0, chunks : 2 * chunks, :] = lax.rsqrt(variance + epsilon)
+
+    mine = lax.broadcasted_iota(jnp.int32, (LANGS, LANE), 0) == lang
+
+    def act_step(i, carry):
+        t = tile(i)
+        average = stat_res[0, pl.ds(i, 1), :]
+        inverse = stat_res[0, pl.ds(chunks + i, 1), :]
+        gain = jnp.sum(jnp.where(mine, gain_ref[:, t], 0.0), axis=0, keepdims=True)
+        bias = jnp.sum(jnp.where(mine, bias_ref[:, t], 0.0), axis=0, keepdims=True)
+        norm = (normed[:, t] - average) * inverse
+        pre = norm * gain + bias
+        s = jax.nn.sigmoid(pre)
+        normed[:, t] = norm
+        slope[:, t] = valid * s * (1.0 + pre * (1.0 - s)) * gain
+        act[:, t] = (pre * s * valid).astype(jnp.bfloat16)
+        return carry
+
+    lax.fori_loop(0, chunks, act_step, 0)
+
+    group = channels // 4
+    rows = wg_ref.shape[0]
+    for g in range(4):
+        turned = jnp.transpose(act[:, g * group : (g + 1) * group].astype(jnp.float32))
+        act_t[g // 2, g % 2] = turned.astype(jnp.bfloat16).reshape(4, 2, rows, frames)
+
+    factors = [
+        push(act_t.at[:, cc, :, xx], ag.at[slot], peer)
+        for slot, cc, xx, peer in ((1, c, xn, to_x), (2, cn, x, to_c), (3, cn, xn, to_cx))
+    ]
+    ag[0] = act_t[:, c, :, x]
+
+    mid = channels // 2
+    w_x.wait_recv()
+    w_yd = push(wfull.at[dp, :, xn, :, mid:], wfull.at[dp, :, xn, :, mid:], to_y)
+    w_core.append(push(wfull.at[dp, :, xn], wfull.at[dp, :, xn], to_c))
+    w_y.wait_recv()
+    w_xd = push(wfull.at[dp_y, :, x, :, :mid], wfull.at[dp_y, :, x, :, :mid], to_x)
+    w_core.append(push(wfull.at[dp_y, :, x], wfull.at[dp_y, :, x], to_c))
+
+    cot_c.wait_recv()
+    cot_cx.wait_recv()
+    for copy in factors:
+        copy.wait_recv()
+    lhs = jnp.concatenate([ag[s].reshape(8 * rows, frames) for s in range(4)], axis=1)
+    rhs = cotg.reshape(4 * frames, channels)
+
+    def grad_step(i, carry):
+        t = pl.ds(pl.multiple_of(i * 256, 256), 256)
+        value = jnp.dot(lhs, rhs[:, t], preferred_element_type=jnp.float32)
+        part[:, :, :, t] = value.astype(jnp.bfloat16).reshape(2, 4, rows, 256)
+        return carry
+
+    lax.fori_loop(0, channels // 256, grad_step, 0)
+    order = z_peers + [z]
+    over_y = [
+        push(part.at[yn, zp], yin.at[d], to_y) for d, zp in enumerate(order)
+    ]
+
+    w_xd.wait_recv()
+    w_yd.wait_recv()
+    w_core.append(push(wfull.at[dp_y, :, xn], wfull.at[dp_y, :, xn], to_c))
+
+    over_z = []
+    for d, zp in enumerate(order):
+        over_y[d].wait_recv()
+        added = part[y, zp].astype(jnp.float32) + yin[d].astype(jnp.float32)
+        if d < 3:
+            ysum[d] = added.astype(jnp.bfloat16)
+            over_z.append(push(ysum.at[d], zin.at[d], (dp, zp * 2 + x)))
+        else:
+            wg_ref[...] = added
+
+    for copy in w_core:
+        copy.wait_recv()
+    weight = wfull.reshape(channels, channels)
+
+    def back_step(i, carry):
+        t = pl.ds(pl.multiple_of(i * 256, 256), 256)
+        back = lax.dot_general(
+            cot_ref[...], weight[t, :], (((1,), (1,)), ((), ())),
+            preferred_element_type=jnp.float32,
+        )
+        grad = back * slope[:, t]
+        slope[:, t] = grad
+        one = jnp.sum(grad, axis=0, keepdims=True)
+        two = jnp.sum(grad * normed[:, t], axis=0, keepdims=True)
+        for j in range(2):
+            cut = slice(j * LANE, (j + 1) * LANE)
+            stat[1, pl.ds(2 * i + j, 1), :] = one[:, cut]
+            stat[1, pl.ds(chunks + 2 * i + j, 1), :] = two[:, cut]
+        return carry
+
+    lax.fori_loop(0, channels // 256, back_step, 0)
+    second = sum_seq(1)
+
+    def out_step(i, carry):
+        t = pl.ds(pl.multiple_of(i * 256, 256), 256)
+        value = jnp.dot(act[...], weight[:, t], preferred_element_type=jnp.float32)
+        out_ref[:, t] = value.astype(jnp.bfloat16)
+        return carry
+
+    lax.fori_loop(0, channels // 256, out_step, 0)
+    second = sum_dp(1, second)
+    stat_res[1] = finish(1, second)
+
+    def grad_conv_step(i, carry):
+        t = tile(i)
+        inverse = stat_res[0, pl.ds(chunks + i, 1), :]
+        shift = stat_res[1, pl.ds(i, 1), :]
+        scale = stat_res[1, pl.ds(chunks + i, 1), :]
+        grad = valid * inverse * (slope[:, t] - shift - normed[:, t] * scale)
+        gext[half : half + frames, t] = grad.astype(jnp.bfloat16)
+        return carry
+
+    lax.fori_loop(0, chunks, grad_conv_step, 0)
+    halo = [
+        push(gext.at[frames : frames + half], gext.at[0:half], seq_up),
+        push(gext.at[half : 2 * half], gext.at[half + frames : frames + 2 * half], seq_down),
+    ]
+    total = wg_ref[...]
+    for d, copy in enumerate(over_z):
+        copy.wait_recv()
+        total = total + zin[d].astype(jnp.float32)
+    wg_ref[...] = total
+    for copy in halo:
+        copy.wait_recv()
+
+    def input_step(i, carry):
+        t = tile(i)
+        xf[:, t] = jnp.where(inside, gext[:, t].astype(jnp.float32), 0.0)
+        weights = tap_ref[:, t]
+        total = jnp.zeros((frames, LANE), jnp.float32)
+        for k in range(taps):
+            total = total + xf[2 * half - k : 2 * half - k + frames, t] * weights[k : k + 1]
+        ig_ref[:, t] = (total * valid).astype(jnp.bfloat16)
+        return carry
+
+    lax.fori_loop(0, chunks, input_step, 0)
+    for copy in pending:
+        copy.wait_send()
+
+
+COPIES = 64
+
+
+def on_device_fused(glu_out, conv_weight, bn_gain, bn_bias, w_out, cotangent, language, length):
+    _, frames, channels = glu_out.shape
+    rows = w_out.shape[0]
+    half = conv_weight.shape[0] // 2
+    bf16, f32 = jnp.bfloat16, jnp.float32
+    stats = 2 * channels // LANE
+    vmem = pl.BlockSpec(memory_space=pltpu.VMEM)
+    smem = pl.BlockSpec(memory_space=pltpu.SMEM)
+    block_out, weight_grad, input_grad = pl.pallas_call(
+        fused,
+        out_shape=(
+            jax.ShapeDtypeStruct((frames, channels), bf16),
+            jax.ShapeDtypeStruct((rows, channels), f32),
+            jax.ShapeDtypeStruct((frames, channels), bf16),
+        ),
+        in_specs=[smem, smem] + [vmem] * 6,
+        out_specs=(vmem, vmem, vmem),
+        scratch_shapes=[
+            pltpu.VMEM((4, 4, 2, rows, channels), bf16),
+            pltpu.VMEM((4, frames, channels), bf16),
+            pltpu.VMEM((frames, channels), bf16),
+            pltpu.VMEM((2, 2, 4, 2, rows, frames), bf16),
+            pltpu.VMEM((4, 2, 4, rows, frames), bf16),
+            pltpu.VMEM((2, 4, rows, channels), bf16),
+            pltpu.VMEM((3, rows, channels), bf16),
+            pltpu.VMEM((4, rows, channels), bf16),
+            pltpu.VMEM((3, rows, channels), bf16),
+            pltpu.VMEM((frames + 2 * half, channels), bf16),
+            pltpu.VMEM((frames + 2 * half, channels), f32),
+            pltpu.VMEM((frames, channels), f32),
+            pltpu.VMEM((frames, channels), f32),
+            pltpu.VMEM((frames + 2 * half, channels), bf16),
+            pltpu.VMEM((16, LANE), jnp.int32),
+            pltpu.VMEM((3, 16, LANE), jnp.int32),
+            pltpu.VMEM((2, stats, LANE), f32),
+            pltpu.VMEM((2, 7, stats, LANE), f32),
+            pltpu.VMEM((2, stats, LANE), f32),
+            pltpu.VMEM((2, 3, stats, LANE), f32),
+            pltpu.VMEM((2, stats, LANE), f32),
+            pltpu.SemaphoreType.DMA((COPIES,)),
+            pltpu.SemaphoreType.DMA((COPIES,)),
+        ],
+        compiler_params=pltpu.CompilerParams(
+            collective_id=0, has_side_effects=True, vmem_limit_bytes=48 * 1024 * 1024
+        ),
+    )(language, length, glu_out[0], conv_weight, bn_gain, bn_bias, w_out, cotangent[0])
+    return block_out[None], weight_grad, input_grad[None]
+
+
 def solution(mesh):
     placed = (
         P("dp", "seq", None),
@@ -117,8 +442,9 @@
         P("dp"),
         P("dp"),
     )
+    small = mesh.shape["dp"] == 4 and mesh.shape["seq"] == 8
     return jax.shard_map(
-        on_device,
+        on_device_fused if small else on_device,
         mesh=mesh,
         in_specs=placed,
         out_specs=(P("dp", "seq", None), P(("dp", "seq"), None), P("dp", "seq", None)),

time: 497 us -> 89.8 us (0.18)
  waiting for transfers between devices: 391 us -> 0 us
  Pallas kernels: 0 us -> 79.7 us
  blocking collectives: 41.5 us -> 0 us
  matrix products: 20 us -> 0 us
  between operations: 15.3 us -> 1.95 us
  other arithmetic: 12.5 us -> 0 us
  starting transfers between devices: 12.1 us -> 0 us
    psum x2 -> x0, waiting for transfers between devices: 199 us -> none  [the longest x1 118 us: on_device(): lax.psum((per_language(one_hot, jnp.sum(grad_normed, axis=1)), per_langua...]
    reduce_scatter x1 -> x0, waiting for transfers between devices: 126 us -> none  [on_device(): lax.psum_scatter(lax.dot_general(flat_active, flat_grad, (((0,), (0,)), (...]
    pallas_call x0 -> x1, Pallas kernels: none -> 79.7 us  [on_device_fused(): pl.pallas_call(fused, out_shape=(jax.ShapeDtypeStruct((frames, channels),...]
    all_gather x1 -> x0, waiting for transfers between devices: 65.3 us -> none  [on_device(): full_weight = lax.all_gather(w_out, ('dp', 'seq'), axis=0, tiled=True)]
    psum x1 -> x0, blocking collectives: 41.5 us -> none  [on_device(): lax.psum((local_sum, local_square, counts), ('dp', 'seq'))]
    dot_general x9 -> x0, matrix products: 20 us -> none  [the longest x6 6.71 us: per_utterance(): jnp.dot(one_hot, values_table, precision=lax.Precision.HIGHEST)[:, None, :]]
    ppermute x4 -> x0, starting transfers between devices: 12 us -> none  [the longest x2 9.39 us: with_halo(): before = lax.ppermute(last, axis, up)]
    unnamed x2 -> x15, local copies, waits for them, and re-layouts: 0.01 us -> 7.81 us
  transfers between devices with their start and end apart: 8 -> 0, of which waited for: 5 -> 0; matrix products, arithmetic and copies ran while one was open for 5% -> 0% of each run, Pallas kernels for 0% -> 0%
where the time goes in v1:
time: 89.8 us; the launch traced here: 89.5 us
  Pallas kernels  79.7 us (89%)
  local copies, waits for them, and re-layouts  7.81 us (9%)
  between operations  1.95 us (2%)
    pallas_call x1, Pallas kernels, on_device_fused(): pl.pallas_call(fused, out_shape=(jax.ShapeDtypeStruct((frames, channels),...  79.7 us
    unnamed x15, local copies, waits for them, and re-layouts  7.81 us

profile of v1, /device:TPU:0, one launch (start us, length us, event | category | flops | bytes accessed | tf_op | source)
XLA Modules:
  0.0 89.5 jit_solution(261491594585435705)
XLA Ops:
  1.9 0.0 copy-start
  1.9 1.0 %copy-done = bf16[1,128,1536]{2,1,0:T(8,128)(2,1)S(1)} copy-done((bf16[1,128,1536]{2,1,0:T(8,128)(2,1)S(1)}, bf16[1,128,1536]{2,1,0:T(8,128)(2,1)}, u32[]{:S(2)}) %copy-start) | copy-done | bytes 393240
  2.9 0.0 copy-start.1
  2.9 1.0 %copy-done.1 = bf16[1,128,1536]{2,1,0:T(8,128)(2,1)S(1)} copy-done((bf16[1,128,1536]{2,1,0:T(8,128)(2,1)S(1)}, bf16[1,128,1536]{2,1,0:T(8,128)(2,1)}, u32[]{:S(2)}) %copy-start.1) | copy-done | bytes 393240
  3.9 0.0 copy-start.2
  3.9 0.9 %copy-done.2 = f32[32,1536]{1,0:T(8,128)S(1)} copy-done((f32[32,1536]{1,0:T(8,128)S(1)}, f32[32,1536]{1,0:T(8,128)}, u32[]{:S(2)}) %copy-start.2) | copy-done | bytes 196632
  4.8 0.0 copy-start.3
  4.8 0.9 %copy-done.3 = bf16[48,1536]{1,0:T(8,128)(2,1)S(1)} copy-done((bf16[48,1536]{1,0:T(8,128)(2,1)S(1)}, bf16[48,1536]{1,0:T(8,128)(2,1)}, u32[]{:S(2)}) %copy-start.3) | copy-done | bytes 147480
  5.8 0.0 copy-start.4
  5.8 0.9 copy-done.4
  6.6 0.0 copy-start.5
  6.7 0.9 copy-done.5
  7.5 79.7 %shard_map.103 = (bf16[128,1536]{1,0:T(8,128)(2,1)S(1)}, f32[48,1536]{1,0:T(8,128)S(1)}, bf16[128,1536]{1,0:T(8,128)(2,1)S(1)}) custom-call(s32[1]{0:T(128)S(6)} %copy.14.lang_ref, s32[1]{0:T(128)S(6)} %copy.15.len_ref, bf16[128,1536]{1,0:T(8,128)(2,1)S(1)} %bitcast.6, f32[32,1536]{1,0:T(8,128)S(1)} %copy-done.2, f32[16,1536]{1,0:T(8,128)S(1)} %copy-done.4, ...), custom_call_target="tpu_custom_call" | custom-call | tf_op jit(solution)/shard_map/pallas_call | solution.py:393
  87.3 0.7 copy.16
  88.0 0.7 copy.17
  88.7 0.7 copy.18
Async XLA Ops:
  1.9 1.0 %copy-start = (bf16[1,128,1536]{2,1,0:T(8,128)(2,1)S(1)}, bf16[1,128,1536]{2,1,0:T(8,128)(2,1)}, u32[]{:S(2)}) copy-start(bf16[1,128,1536]{2,1,0:T(8,128)(2,1)} %param.8) | copy-start | bytes 1179652
  2.9 1.0 %copy-start.1 = (bf16[1,128,1536]{2,1,0:T(8,128)(2,1)S(1)}, bf16[1,128,1536]{2,1,0:T(8,128)(2,1)}, u32[]{:S(2)}) copy-start(bf16[1,128,1536]{2,1,0:T(8,128)(2,1)} %param.13) | copy-start | bytes 1179652
  3.9 0.9 %copy-start.2 = (f32[32,1536]{1,0:T(8,128)S(1)}, f32[32,1536]{1,0:T(8,128)}, u32[]{:S(2)}) copy-start(f32[32,1536]{1,0:T(8,128)} %tap_ref.1) | copy-start | bytes 589828
  4.8 0.9 %copy-start.3 = (bf16[48,1536]{1,0:T(8,128)(2,1)S(1)}, bf16[48,1536]{1,0:T(8,128)(2,1)}, u32[]{:S(2)}) copy-start(bf16[48,1536]{1,0:T(8,128)(2,1)} %w_ref.1) | copy-start | bytes 442372
  5.8 0.9 copy-start.4
  6.6 0.9 copy-start.5

commit v2 on v1

--- a/solution.py
+++ b/solution.py
@@ -117,14 +117,15 @@
 
 
 def fused(
-    lang_ref, len_ref, x_ref, tap_ref, gain_ref, bias_ref, w_ref, cot_ref,
+    lang_ref, len_ref, x_hbm, tap_hbm, gain_hbm, bias_hbm, w_hbm, cot_hbm,
     out_ref, wg_ref, ig_ref,
-    wfull, cotg, act, act_t, ag, part, ysum, yin, zin,
+    tap_ref, gain_ref, bias_ref, wgrp, cotg, act, act_t, ag, acts, back_t, back_out,
+    opart, oin, osum, osend, ox, part, ysum, yin, zin,
     ext, xf, normed, slope, gext,
     info, info_in, stat, stat_in, stat_mid, stat_dp, stat_res,
-    send, recv,
+    local, send, recv,
 ):
-    frames, channels = x_ref.shape
+    frames, channels = x_hbm.shape
     taps = tap_ref.shape[0]
     half = taps // 2
     chunks = channels // LANE
@@ -143,10 +144,23 @@
     for peer in greet:
         pl.semaphore_signal(barrier, inc=1, device_id=peer, device_id_type=MESH)
 
+    own = [
+        pltpu.make_async_copy(src, dst, local.at[i])
+        for i, (src, dst) in enumerate((
+            (x_hbm, ext.at[half : half + frames]),
+            (w_hbm, wgrp.at[y, z]),
+            (cot_hbm, cotg.at[0]),
+            (tap_hbm, tap_ref),
+            (gain_hbm, gain_ref),
+            (bias_hbm, bias_ref),
+        ))
+    ]
+    for copy in own:
+        copy.start()
     info[0:8, :] = jnp.full((8, LANE), lang, jnp.int32)
     info[8:16, :] = jnp.full((8, LANE), length, jnp.int32)
-    wfull[dp, z, x] = w_ref[...]
-    cotg[0] = cot_ref[...]
+    for copy in own:
+        copy.wait()
     pl.semaphore_wait(barrier, len(greet))
 
     pending = []
@@ -165,19 +179,19 @@
 
     seq_up, seq_down = (dp, (seq + 1) % 8), (dp, (seq + 7) % 8)
     halo = [
-        push(x_ref.at[frames - half : frames], ext.at[0:half], seq_up),
-        push(x_ref.at[0:half], ext.at[half + frames : frames + 2 * half], seq_down),
+        push(ext.at[frames : frames + half], ext.at[0:half], seq_up),
+        push(ext.at[half : 2 * half], ext.at[half + frames : frames + 2 * half], seq_down),
     ]
-    w_z = [push(w_ref, wfull.at[dp, z, x], (dp, zp * 2 + x)) for zp in z_peers]
-    cot_x = push(cot_ref, cotg.at[1], to_x)
-    cot_c = push(cot_ref, cotg.at[2], to_c)
+    w_z = [push(wgrp.at[y, z], wgrp.at[y, z], (dp, zp * 2 + x)) for zp in z_peers]
+    w_y = [push(wgrp.at[y, z], wgrp.at[y, z], to_y)]
+    cot_x = push(cotg.at[0], cotg.at[1], to_x)
+    cot_c = push(cotg.at[0], cotg.at[2], to_c)
     told = [push(info, info_in.at[d], peer) for d, peer in enumerate(dp_peers)]
 
     row = lax.broadcasted_iota(jnp.int32, (frames + 2 * half, LANE), 0) + (seq * frames - half)
     inside = (row >= 0) & (row < length)
     valid = inside[half : half + frames].astype(jnp.float32)
 
-    ext[half : half + frames, :] = x_ref[...]
     for copy in halo:
         copy.wait_recv()
 
@@ -221,13 +235,11 @@
 
     first = sum_seq(0)
 
-    for copy in w_z:
-        copy.wait_recv()
-    w_x = push(wfull.at[dp, :, x], wfull.at[dp, :, x], to_x)
-    w_y = push(wfull.at[dp, :, x], wfull.at[dp, :, x], to_y)
-    w_core = [push(wfull.at[dp, :, x], wfull.at[dp, :, x], to_c)]
-
     first = sum_dp(0, first)
+    for d in range(3):
+        w_z[d].wait_recv()
+        block = wgrp.at[y, (z + 3 - d) % 4]
+        w_y.append(push(block, block, to_y))
     cot_x.wait_recv()
     cot_cx = push(cotg.at[1], cotg.at[3], to_c)
     for copy in told:
@@ -268,14 +280,6 @@
     ]
     ag[0] = act_t[:, c, :, x]
 
-    mid = channels // 2
-    w_x.wait_recv()
-    w_yd = push(wfull.at[dp, :, xn, :, mid:], wfull.at[dp, :, xn, :, mid:], to_y)
-    w_core.append(push(wfull.at[dp, :, xn], wfull.at[dp, :, xn], to_c))
-    w_y.wait_recv()
-    w_xd = push(wfull.at[dp_y, :, x, :, :mid], wfull.at[dp_y, :, x, :, :mid], to_x)
-    w_core.append(push(wfull.at[dp_y, :, x], wfull.at[dp_y, :, x], to_c))
-
     cot_c.wait_recv()
     cot_cx.wait_recv()
     for copy in factors:
@@ -295,51 +299,68 @@
         push(part.at[yn, zp], yin.at[d], to_y) for d, zp in enumerate(order)
     ]
 
-    w_xd.wait_recv()
-    w_yd.wait_recv()
-    w_core.append(push(wfull.at[dp_y, :, xn], wfull.at[dp_y, :, xn], to_c))
-
-    over_z = []
-    for d, zp in enumerate(order):
-        over_y[d].wait_recv()
-        added = part[y, zp].astype(jnp.float32) + yin[d].astype(jnp.float32)
-        if d < 3:
-            ysum[d] = added.astype(jnp.bfloat16)
-            over_z.append(push(ysum.at[d], zin.at[d], (dp, zp * 2 + x)))
+    for copy in w_y:
+        copy.wait_recv()
+    weight = wgrp.reshape(8 * rows, channels)
+    where = ((0, c, x, None), (1, c, xn, to_x), (2, cn, x, to_c), (3, cn, xn, to_cx))
+    backs = []
+    for slot, cc, xx, peer in where:
+        value = lax.dot_general(
+            weight[...], cotg[slot], (((1,), (1,)), ((), ())),
+            preferred_element_type=jnp.float32,
+        ).astype(jnp.bfloat16).reshape(2, 4, rows, frames)
+        if peer is None:
+            back_t[:, c, :, x] = value
         else:
-            wg_ref[...] = added
-
-    for copy in w_core:
-        copy.wait_recv()
-    weight = wfull.reshape(channels, channels)
-
-    def back_step(i, carry):
+            back_out[slot - 1] = value
+            backs.append(push(back_out.at[slot - 1], back_t.at[:, c, :, x], peer))
+
+    acts[...] = jnp.transpose(lhs.astype(jnp.float32)).astype(jnp.bfloat16)
+
+    def out_step(i, carry):
         t = pl.ds(pl.multiple_of(i * 256, 256), 256)
-        back = lax.dot_general(
-            cot_ref[...], weight[t, :], (((1,), (1,)), ((), ())),
-            preferred_element_type=jnp.float32,
-        )
-        grad = back * slope[:, t]
+        value = jnp.dot(acts[...], weight[:, t], preferred_element_type=jnp.float32)
+        opart[:, :, t] = value.astype(jnp.bfloat16).reshape(4, frames, 256)
+        return carry
+
+    lax.fori_loop(0, channels // 256, out_step, 0)
+    out_c = push(opart.at[2:4], oin, to_c)
+
+    for copy in backs:
+        copy.wait_recv()
+    for g in range(4):
+        t = slice(g * group, (g + 1) * group)
+        piece = back_t[g // 2, g % 2].reshape(group, frames).astype(jnp.float32)
+        grad = jnp.transpose(piece) * slope[:, t]
         slope[:, t] = grad
         one = jnp.sum(grad, axis=0, keepdims=True)
         two = jnp.sum(grad * normed[:, t], axis=0, keepdims=True)
-        for j in range(2):
+        for j in range(group // LANE):
             cut = slice(j * LANE, (j + 1) * LANE)
-            stat[1, pl.ds(2 * i + j, 1), :] = one[:, cut]
-            stat[1, pl.ds(chunks + 2 * i + j, 1), :] = two[:, cut]
-        return carry
-
-    lax.fori_loop(0, channels // 256, back_step, 0)
+            at = g * (group // LANE) + j
+            stat[1, at : at + 1, :] = one[:, cut]
+            stat[1, chunks + at : chunks + at + 1, :] = two[:, cut]
     second = sum_seq(1)
 
-    def out_step(i, carry):
-        t = pl.ds(pl.multiple_of(i * 256, 256), 256)
-        value = jnp.dot(act[...], weight[:, t], preferred_element_type=jnp.float32)
-        out_ref[:, t] = value.astype(jnp.bfloat16)
-        return carry
-
-    lax.fori_loop(0, channels // 256, out_step, 0)
+    out_c.wait_recv()
+    osend[...] = (opart[1].astype(jnp.float32) + oin[1].astype(jnp.float32)).astype(jnp.bfloat16)
+    out_x = push(osend, ox, to_x)
+    osum[...] = opart[0].astype(jnp.float32) + oin[0].astype(jnp.float32)
+
+    over_z = []
+
+    def pass_on(d):
+        over_y[d].wait_recv()
+        added = part[y, order[d]].astype(jnp.float32) + yin[d].astype(jnp.float32)
+        if d < 3:
+            ysum[d] = added.astype(jnp.bfloat16)
+            over_z.append(push(ysum.at[d], zin.at[d], (dp, order[d] * 2 + x)))
+        else:
+            wg_ref[...] = added
+
+    pass_on(0)
     second = sum_dp(1, second)
+    pass_on(1)
     stat_res[1] = finish(1, second)
 
     def grad_conv_step(i, carry):
@@ -356,11 +377,8 @@
         push(gext.at[frames : frames + half], gext.at[0:half], seq_up),
         push(gext.at[half : 2 * half], gext.at[half + frames : frames + 2 * half], seq_down),
     ]
-    total = wg_ref[...]
-    for d, copy in enumerate(over_z):
-        copy.wait_recv()
-        total = total + zin[d].astype(jnp.float32)
-    wg_ref[...] = total
+    pass_on(2)
+    pass_on(3)
     for copy in halo:
         copy.wait_recv()
 
@@ -375,6 +393,13 @@
         return carry
 
     lax.fori_loop(0, chunks, input_step, 0)
+    out_x.wait_recv()
+    out_ref[...] = (osum[...] + ox[...].astype(jnp.float32)).astype(jnp.bfloat16)
+    total = wg_ref[...]
+    for d, copy in enumerate(over_z):
+        copy.wait_recv()
+        total = total + zin[d].astype(jnp.float32)
+    wg_ref[...] = total
     for copy in pending:
         copy.wait_send()
 
@@ -397,14 +422,25 @@
             jax.ShapeDtypeStruct((rows, channels), f32),
             jax.ShapeDtypeStruct((frames, channels), bf16),
         ),
-        in_specs=[smem, smem] + [vmem] * 6,
+        in_specs=[smem, smem] + [pl.BlockSpec(memory_space=pltpu.HBM)] * 6,
         out_specs=(vmem, vmem, vmem),
         scratch_shapes=[
-            pltpu.VMEM((4, 4, 2, rows, channels), bf16),
+            pltpu.VMEM(conv_weight.shape, f32),
+            pltpu.VMEM(bn_gain.shape, f32),
+            pltpu.VMEM(bn_bias.shape, f32),
+            pltpu.VMEM((2, 4, rows, channels), bf16),
             pltpu.VMEM((4, frames, channels), bf16),
             pltpu.VMEM((frames, channels), bf16),
             pltpu.VMEM((2, 2, 4, 2, rows, frames), bf16),
             pltpu.VMEM((4, 2, 4, rows, frames), bf16),
+            pltpu.VMEM((4 * frames, channels // 4), bf16),
+            pltpu.VMEM((2, 2, 4, 2, rows, frames), bf16),
+            pltpu.VMEM((3, 2, 4, rows, frames), bf16),
+            pltpu.VMEM((4, frames, channels), bf16),
+            pltpu.VMEM((2, frames, channels), bf16),
+            pltpu.VMEM((frames, channels), f32),
+            pltpu.VMEM((frames, channels), bf16),
+            pltpu.VMEM((frames, channels), bf16),
             pltpu.VMEM((2, 4, rows, channels), bf16),
             pltpu.VMEM((3, rows, channels), bf16),
             pltpu.VMEM((4, rows, channels), bf16),
@@ -421,11 +457,12 @@
             pltpu.VMEM((2, stats, LANE), f32),
             pltpu.VMEM((2, 3, stats, LANE), f32),
             pltpu.VMEM((2, stats, LANE), f32),
+            pltpu.SemaphoreType.DMA((6,)),
             pltpu.SemaphoreType.DMA((COPIES,)),
             pltpu.SemaphoreType.DMA((COPIES,)),
         ],
         compiler_params=pltpu.CompilerParams(
-            collective_id=0, has_side_effects=True, vmem_limit_bytes=48 * 1024 * 1024
+            collective_id=0, has_side_effects=True, vmem_limit_bytes=62 * 1024 * 1024
         ),
     )(language, length, glu_out[0], conv_weight, bn_gain, bn_bias, w_out, cotangent[0])
     return block_out[None], weight_grad, input_grad[None]

time: 89.8 us -> 69.6 us (0.78)
  the two profiles are of different devices: /device:TPU:0 before, /device:TPU:16 now
where the time goes in v2:
time: 69.6 us; the launch traced here: 69.4 us
  Pallas kernels  63.8 us (92%)
  local copies, waits for them, and re-layouts  3.66 us (5%)
  between operations  1.94 us (3%)
    pallas_call x1, Pallas kernels, on_device_fused(): pl.pallas_call(fused, out_shape=(jax.ShapeDtypeStruct((frames, channels),...  63.8 us
    unnamed x7, local copies, waits for them, and re-layouts  3.66 us

profile of v2, /device:TPU:16, one launch (start us, length us, event | category | flops | bytes accessed | tf_op | source)
XLA Modules:
  0.0 69.4 jit_solution(12432515820883572653)
XLA Ops:
  1.9 63.8 %shard_map.103 = (bf16[128,1536]{1,0:T(8,128)(2,1)}, f32[48,1536]{1,0:T(8,128)}, bf16[128,1536]{1,0:T(8,128)(2,1)}) custom-call(s32[1]{0:T(128)S(6)} %copy.14.lang_ref, s32[1]{0:T(128)S(6)} %copy.15.len_ref, bf16[128,1536]{1,0:T(8,128)(2,1)} %bitcast.6, f32[32,1536]{1,0:T(8,128)} %tap_hbm.1, f32[16,1536]{1,0:T(8,128)} %gain_hbm.1, f32[16,1536]{1,0:T(8,128)} %bias_hbm.1, ...), custom_call_target="tpu_custom_call" | custom-call | tf_op jit(solution)/shard_map/pallas_call | solution.py:418
  65.7 0.0 copy-start.1
  65.7 1.8 %copy.16 = bf16[1,128,1536]{2,1,0:T(8,128)(2,1)} copy(bf16[1,128,1536]{2,1,0:T(8,128)(2,1)} %bitcast.5) | data formatting | bytes 786432
  67.5 0.0 copy-done.1
  67.5 0.0 copy-start
  67.5 0.7 %copy.17 = f32[48,1536]{1,0:T(8,128)} copy(f32[48,1536]{1,0:T(8,128)S(1)} %copy-done.1) | data formatting | bytes 589824
  68.3 0.4 copy-done
  68.6 0.7 %copy.18 = bf16[1,128,1536]{2,1,0:T(8,128)(2,1)} copy(bf16[1,128,1536]{2,1,0:T(8,128)(2,1)S(1)} %bitcast.4) | data formatting | bytes 786432
Async XLA Ops:
  65.7 1.8 %copy-start.1 = (f32[48,1536]{1,0:T(8,128)S(1)}, f32[48,1536]{1,0:T(8,128)}, u32[]{:S(2)}) copy-start(f32[48,1536]{1,0:T(8,128)} %get-tuple-element.13) | copy-start | bytes 884740
  67.5 1.1 %copy-start = (bf16[128,1536]{1,0:T(8,128)(2,1)S(1)}, bf16[128,1536]{1,0:T(8,128)(2,1)}, u32[]{:S(2)}) copy-start(bf16[128,1536]{1,0:T(8,128)(2,1)} %get-tuple-element.8) | copy-start | bytes 1179652

commit v3 on v2

--- a/solution.py
+++ b/solution.py
@@ -118,6 +118,7 @@
 
 def fused(
     lang_ref, len_ref, x_hbm, tap_hbm, gain_hbm, bias_hbm, w_hbm, cot_hbm,
+    out_hbm, wg_hbm, ig_hbm,
     out_ref, wg_ref, ig_ref,
     tap_ref, gain_ref, bias_ref, wgrp, cotg, act, act_t, ag, acts, back_t, back_out,
     opart, oin, osum, osend, ox, part, ysum, yin, zin,
@@ -326,6 +327,19 @@
     lax.fori_loop(0, channels // 256, out_step, 0)
     out_c = push(opart.at[2:4], oin, to_c)
 
+    over_z = []
+
+    def pass_on(d):
+        over_y[d].wait_recv()
+        added = part[y, order[d]].astype(jnp.float32) + yin[d].astype(jnp.float32)
+        if d < 3:
+            ysum[d] = added.astype(jnp.bfloat16)
+            over_z.append(push(ysum.at[d], zin.at[d], (dp, order[d] * 2 + x)))
+        else:
+            wg_ref[...] = added
+
+    pass_on(0)
+
     for copy in backs:
         copy.wait_recv()
     for g in range(4):
@@ -347,20 +361,9 @@
     out_x = push(osend, ox, to_x)
     osum[...] = opart[0].astype(jnp.float32) + oin[0].astype(jnp.float32)
 
-    over_z = []
-
-    def pass_on(d):
-        over_y[d].wait_recv()
-        added = part[y, order[d]].astype(jnp.float32) + yin[d].astype(jnp.float32)
-        if d < 3:
-            ysum[d] = added.astype(jnp.bfloat16)
-            over_z.append(push(ysum.at[d], zin.at[d], (dp, order[d] * 2 + x)))
-        else:
-            wg_ref[...] = added
-
-    pass_on(0)
+    pass_on(1)
     second = sum_dp(1, second)
-    pass_on(1)
+    pass_on(2)
     stat_res[1] = finish(1, second)
 
     def grad_conv_step(i, carry):
@@ -377,8 +380,11 @@
         push(gext.at[frames : frames + half], gext.at[0:half], seq_up),
         push(gext.at[half : 2 * half], gext.at[half + frames : frames + 2 * half], seq_down),
     ]
-    pass_on(2)
     pass_on(3)
+    out_x.wait_recv()
+    out_ref[...] = (osum[...] + ox[...].astype(jnp.float32)).astype(jnp.bfloat16)
+    leave = [pltpu.make_async_copy(out_ref, out_hbm, local.at[0])]
+    leave[0].start()
     for copy in halo:
         copy.wait_recv()
 
@@ -392,19 +398,38 @@
         ig_ref[:, t] = (total * valid).astype(jnp.bfloat16)
         return carry
 
-    lax.fori_loop(0, chunks, input_step, 0)
-    out_x.wait_recv()
-    out_ref[...] = (osum[...] + ox[...].astype(jnp.float32)).astype(jnp.bfloat16)
+    for g in range(4):
+        lax.fori_loop(g * chunks // 4, (g + 1) * chunks // 4, input_step, 0)
+        t = pl.ds(g * group, group)
+        leave.append(pltpu.make_async_copy(ig_ref.at[:, t], ig_hbm.at[:, t], local.at[1 + g]))
+        leave[-1].start()
     total = wg_ref[...]
     for d, copy in enumerate(over_z):
         copy.wait_recv()
         total = total + zin[d].astype(jnp.float32)
     wg_ref[...] = total
+    leave.append(pltpu.make_async_copy(wg_ref, wg_hbm, local.at[5]))
+    leave[-1].start()
+    for copy in leave:
+        copy.wait()
     for copy in pending:
         copy.wait_send()
 
 
 COPIES = 64
+
+
+def hand_over(a_in, b_in, c_in, a_out, b_out, c_out, sems):
+    copies = []
+    for src, dst in ((a_in, a_out), (b_in, b_out), (c_in, c_out)):
+        step = src.shape[0] // 3 if src.shape[0] % 48 == 0 else src.shape[0] // 4
+        for at in range(0, src.shape[0], step):
+            cut = pl.ds(at, step)
+            copies.append(pltpu.make_async_copy(src.at[cut], dst.at[cut], sems.at[len(copies)]))
+    for copy in copies:
+        copy.start()
+    for copy in copies:
+        copy.wait()
 
 
 def on_device_fused(glu_out, conv_weight, bn_gain, bn_bias, w_out, cotangent, language, length):
@@ -413,18 +438,22 @@
     half = conv_weight.shape[0] // 2
     bf16, f32 = jnp.bfloat16, jnp.float32
     stats = 2 * channels // LANE
-    vmem = pl.BlockSpec(memory_space=pltpu.VMEM)
+    hbm = pl.BlockSpec(memory_space=pltpu.HBM)
     smem = pl.BlockSpec(memory_space=pltpu.SMEM)
-    block_out, weight_grad, input_grad = pl.pallas_call(
+    results = (
+        jax.ShapeDtypeStruct((frames, channels), bf16),
+        jax.ShapeDtypeStruct((rows, channels), f32),
+        jax.ShapeDtypeStruct((frames, channels), bf16),
+    )
+    made = pl.pallas_call(
         fused,
-        out_shape=(
-            jax.ShapeDtypeStruct((frames, channels), bf16),
-            jax.ShapeDtypeStruct((rows, channels), f32),
-            jax.ShapeDtypeStruct((frames, channels), bf16),
-        ),
-        in_specs=[smem, smem] + [pl.BlockSpec(memory_space=pltpu.HBM)] * 6,
-        out_specs=(vmem, vmem, vmem),
+        out_shape=results,
+        in_specs=[smem, smem] + [hbm] * 6,
+        out_specs=(hbm, hbm, hbm),
         scratch_shapes=[
+            pltpu.VMEM((frames, channels), bf16),
+            pltpu.VMEM((rows, channels), f32),
+            pltpu.VMEM((frames, channels), bf16),
             pltpu.VMEM(conv_weight.shape, f32),
             pltpu.VMEM(bn_gain.shape, f32),
             pltpu.VMEM(bn_bias.shape, f32),
@@ -465,6 +494,14 @@
             collective_id=0, has_side_effects=True, vmem_limit_bytes=62 * 1024 * 1024
         ),
     )(language, length, glu_out[0], conv_weight, bn_gain, bn_bias, w_out, cotangent[0])
+    block_out, weight_grad, input_grad = pl.pallas_call(
+        hand_over,
+        out_shape=results,
+        in_specs=[hbm] * 3,
+        out_specs=(hbm, hbm, hbm),
+        scratch_shapes=[pltpu.SemaphoreType.DMA((12,))],
+        compiler_params=pltpu.CompilerParams(vmem_limit_bytes=62 * 1024 * 1024),
+    )(*made)
     return block_out[None], weight_grad, input_grad[None]
 
 

time: 69.6 us -> 105 us (1.51)
  the two profiles are of different devices: /device:TPU:16 before, /device:TPU:0 now
where the time goes in v3:
time: 105 us
  Pallas kernels  103 us (98%)
  between operations  1.93 us (2%)
    pallas_call x1, Pallas kernels, on_device_fused(): pl.pallas_call(fused, out_shape=results, in_specs=[smem, smem] + [hbm] *...  69.3 us
    pallas_call x1, Pallas kernels, on_device_fused(): pl.pallas_call(hand_over, out_shape=results, in_specs=[hbm] * 3, out_spec...  34 us

profile of v3, /device:TPU:0, one launch (start us, length us, event | category | flops | bytes accessed | tf_op | source)
XLA Modules:
  0.0 105.2 jit_solution(14981380283040316857)
XLA Ops:
  1.9 69.3 %shard_map.103 = (bf16[128,1536]{1,0:T(8,128)(2,1)}, f32[48,1536]{1,0:T(8,128)}, bf16[128,1536]{1,0:T(8,128)(2,1)}) custom-call(s32[1]{0:T(128)S(6)} %copy.11.lang_ref, s32[1]{0:T(128)S(6)} %copy.12.len_ref, bf16[128,1536]{1,0:T(8,128)(2,1)} %bitcast.4, f32[32,1536]{1,0:T(8,128)} %tap_hbm.1, f32[16,1536]{1,0:T(8,128)} %gain_hbm.1, f32[16,1536]{1,0:T(8,128)} %bias_hbm.1, ...), custom_call_target="tpu_custom_call" | custom-call | tf_op jit(solution)/shard_map/pallas_call | solution.py:448
  71.2 34.0 %shard_map.104 = (bf16[128,1536]{1,0:T(8,128)(2,1)}, f32[48,1536]{1,0:T(8,128)}, bf16[128,1536]{1,0:T(8,128)(2,1)}) custom-call(bf16[128,1536]{1,0:T(8,128)(2,1)} %get-tuple-element.9.a_in, f32[48,1536]{1,0:T(8,128)} %get-tuple-element.10.b_in, bf16[128,1536]{1,0:T(8,128)(2,1)} %get-tuple-element.11.c_in), custom_call_target="tpu_custom_call" | custom-call | tf_op jit(solution)/shard_map/pallas_call | solution.py:497

commit v4 on v3

--- a/solution.py
+++ b/solution.py
@@ -419,17 +419,10 @@
 COPIES = 64
 
 
-def hand_over(a_in, b_in, c_in, a_out, b_out, c_out, sems):
-    copies = []
-    for src, dst in ((a_in, a_out), (b_in, b_out), (c_in, c_out)):
-        step = src.shape[0] // 3 if src.shape[0] % 48 == 0 else src.shape[0] // 4
-        for at in range(0, src.shape[0], step):
-            cut = pl.ds(at, step)
-            copies.append(pltpu.make_async_copy(src.at[cut], dst.at[cut], sems.at[len(copies)]))
-    for copy in copies:
-        copy.start()
-    for copy in copies:
-        copy.wait()
+def hand_over(a_in, b_in, c_in, a_out, b_out, c_out):
+    a_out[...] = a_in[...]
+    b_out[...] = b_in[...]
+    c_out[...] = c_in[...]
 
 
 def on_device_fused(glu_out, conv_weight, bn_gain, bn_bias, w_out, cotangent, language, length):
@@ -438,6 +431,7 @@
     half = conv_weight.shape[0] // 2
     bf16, f32 = jnp.bfloat16, jnp.float32
     stats = 2 * channels // LANE
+    vmem = pl.BlockSpec(memory_space=pltpu.VMEM)
     hbm = pl.BlockSpec(memory_space=pltpu.HBM)
     smem = pl.BlockSpec(memory_space=pltpu.SMEM)
     results = (
@@ -497,9 +491,8 @@
     block_out, weight_grad, input_grad = pl.pallas_call(
         hand_over,
         out_shape=results,
-        in_specs=[hbm] * 3,
-        out_specs=(hbm, hbm, hbm),
-        scratch_shapes=[pltpu.SemaphoreType.DMA((12,))],
+        in_specs=[vmem] * 3,
+        out_specs=(vmem, vmem, vmem),
         compiler_params=pltpu.CompilerParams(vmem_limit_bytes=62 * 1024 * 1024),
     )(*made)
     return block_out[None], weight_grad, input_grad[None]

time: 105 us -> 73.6 us (0.70)
  Pallas kernels: 103 us -> 71.5 us
    pallas_call x1, Pallas kernels: 34 us -> 2.2 us  [on_device_fused(): pl.pallas_call(hand_over, out_shape=results, in_specs=[vmem] * 3, out_spe...]
where the time goes in v4:
time: 73.6 us; the launch traced here: 73.4 us
  Pallas kernels  71.5 us (97%)
  between operations  1.93 us (3%)
    pallas_call x1, Pallas kernels, on_device_fused(): pl.pallas_call(fused, out_shape=results, in_specs=[smem, smem] + [hbm] *...  69.3 us
    pallas_call x1, Pallas kernels, on_device_fused(): pl.pallas_call(hand_over, out_shape=results, in_specs=[vmem] * 3, out_spe...  2.2 us

profile of v4, /device:TPU:0, one launch (start us, length us, event | category | flops | bytes accessed | tf_op | source)
XLA Modules:
  0.0 73.4 jit_solution(3032448802309336682)
XLA Ops:
  1.9 69.3 %shard_map.103 = (bf16[128,1536]{1,0:T(8,128)(2,1)}, f32[48,1536]{1,0:T(8,128)}, bf16[128,1536]{1,0:T(8,128)(2,1)}) custom-call(s32[1]{0:T(128)S(6)} %copy.11.lang_ref, s32[1]{0:T(128)S(6)} %copy.12.len_ref, bf16[128,1536]{1,0:T(8,128)(2,1)} %bitcast.4, f32[32,1536]{1,0:T(8,128)} %tap_hbm.1, f32[16,1536]{1,0:T(8,128)} %gain_hbm.1, f32[16,1536]{1,0:T(8,128)} %bias_hbm.1, ...), custom_call_target="tpu_custom_call" | custom-call | tf_op jit(solution)/shard_map/pallas_call | solution.py:442
  71.2 2.2 %shard_map.104 = (bf16[128,1536]{1,0:T(8,128)(2,1)}, f32[48,1536]{1,0:T(8,128)}, bf16[128,1536]{1,0:T(8,128)(2,1)}) custom-call(bf16[128,1536]{1,0:T(8,128)(2,1)} %get-tuple-element.9.a_in, f32[48,1536]{1,0:T(8,128)} %get-tuple-element.10.b_in, bf16[128,1536]{1,0:T(8,128)(2,1)} %get-tuple-element.11.c_in), custom_call_target="tpu_custom_call" | custom-call | tf_op jit(solution)/shard_map/pallas_call | solution.py:491

commit v5 on v2

--- a/solution.py
+++ b/solution.py
@@ -326,6 +326,19 @@
     lax.fori_loop(0, channels // 256, out_step, 0)
     out_c = push(opart.at[2:4], oin, to_c)
 
+    over_z = []
+
+    def pass_on(d):
+        over_y[d].wait_recv()
+        added = part[y, order[d]].astype(jnp.float32) + yin[d].astype(jnp.float32)
+        if d < 3:
+            ysum[d] = added.astype(jnp.bfloat16)
+            over_z.append(push(ysum.at[d], zin.at[d], (dp, order[d] * 2 + x)))
+        else:
+            wg_ref[...] = added
+
+    pass_on(0)
+
     for copy in backs:
         copy.wait_recv()
     for g in range(4):
@@ -347,20 +360,9 @@
     out_x = push(osend, ox, to_x)
     osum[...] = opart[0].astype(jnp.float32) + oin[0].astype(jnp.float32)
 
-    over_z = []
-
-    def pass_on(d):
-        over_y[d].wait_recv()
-        added = part[y, order[d]].astype(jnp.float32) + yin[d].astype(jnp.float32)
-        if d < 3:
-            ysum[d] = added.astype(jnp.bfloat16)
-            over_z.append(push(ysum.at[d], zin.at[d], (dp, order[d] * 2 + x)))
-        else:
-            wg_ref[...] = added
-
-    pass_on(0)
+    pass_on(1)
     second = sum_dp(1, second)
-    pass_on(1)
+    pass_on(2)
     stat_res[1] = finish(1, second)
 
     def grad_conv_step(i, carry):
@@ -377,7 +379,6 @@
         push(gext.at[frames : frames + half], gext.at[0:half], seq_up),
         push(gext.at[half : 2 * half], gext.at[half + frames : frames + 2 * half], seq_down),
     ]
-    pass_on(2)
     pass_on(3)
     for copy in halo:
         copy.wait_recv()

time: 69.6 us -> 75.5 us (1.085)
  the two profiles are of different devices: /device:TPU:16 before, /device:TPU:0 now
where the time goes in v5:
time: 75.5 us; the launch traced here: 75.2 us
  Pallas kernels  69.6 us (92%)
  local copies, waits for them, and re-layouts  3.66 us (5%)
  between operations  1.94 us (3%)
    pallas_call x1, Pallas kernels, on_device_fused(): pl.pallas_call(fused, out_shape=(jax.ShapeDtypeStruct((frames, channels),...  69.6 us
    unnamed x7, local copies, waits for them, and re-layouts  3.66 us

profile of v5, /device:TPU:0, one launch (start us, length us, event | category | flops | bytes accessed | tf_op | source)
XLA Modules:
  0.0 75.2 jit_solution(8881743355840358109)
XLA Ops:
  1.9 69.6 %shard_map.103 = (bf16[128,1536]{1,0:T(8,128)(2,1)}, f32[48,1536]{1,0:T(8,128)}, bf16[128,1536]{1,0:T(8,128)(2,1)}) custom-call(s32[1]{0:T(128)S(6)} %copy.14.lang_ref, s32[1]{0:T(128)S(6)} %copy.15.len_ref, bf16[128,1536]{1,0:T(8,128)(2,1)} %bitcast.6, f32[32,1536]{1,0:T(8,128)} %tap_hbm.1, f32[16,1536]{1,0:T(8,128)} %gain_hbm.1, f32[16,1536]{1,0:T(8,128)} %bias_hbm.1, ...), custom_call_target="tpu_custom_call" | custom-call | tf_op jit(solution)/shard_map/pallas_call | solution.py:419
  71.6 0.0 copy-start.1
  71.6 1.8 %copy.16 = bf16[1,128,1536]{2,1,0:T(8,128)(2,1)} copy(bf16[1,128,1536]{2,1,0:T(8,128)(2,1)} %bitcast.5) | data formatting | bytes 786432
  73.4 0.0 copy-done.1
  73.4 0.0 copy-start
  73.4 0.7 copy.17
  74.1 0.4 copy-done
  74.5 0.7 copy.18
Async XLA Ops:
  71.6 1.8 %copy-start.1 = (f32[48,1536]{1,0:T(8,128)S(1)}, f32[48,1536]{1,0:T(8,128)}, u32[]{:S(2)}) copy-start(f32[48,1536]{1,0:T(8,128)} %get-tuple-element.13) | copy-start | bytes 884740
  73.4 1.1 %copy-start = (bf16[128,1536]{1,0:T(8,128)(2,1)S(1)}, bf16[128,1536]{1,0:T(8,128)(2,1)}, u32[]{:S(2)}) copy-start(bf16[128,1536]{1,0:T(8,128)(2,1)} %get-tuple-element.8) | copy-start | bytes 1179652
